TPU v7x, 32 devices: a whole 2x2x4 slice. The times are simulated.
32 devices in a mesh: dp: 4 (over y, x), space: 8 (over z, core).
Axes of the slice: x: 2, y: 2, z: 4, core: 2. Of those that a mesh axis runs over, the one named last changes fastest.
Arguments:
- volumes: bfloat16 [4, 4, 32, 16, 256], P('dp', None, 'space'), may hold values from -6 to 6
- targets: float32 [4, 4], P('dp'), may hold values from -4 to 4
- first_kernel: bfloat16 [16, 4, 3, 3, 3], replicated, may hold values from -1 to 1
- first_bias: float32 [16], replicated, may hold values from -0.54 to -0.43
- second_kernel: bfloat16 [128, 16, 3, 3, 3], replicated, may hold values from -0.3125 to 0.3125
- second_bias: float32 [128], replicated, may hold values from -0.4 to 0.4
- head_weight: float32 [4, 128], replicated, may hold values from -0.5 to 0.5
- head_bias: float32 [4], replicated, may hold values from -3 to 3
Outputs:
- prediction: float32 [4, 4], P('dp')
- grad_first_kernel: float32 [16, 4, 3, 3, 3], replicated
- grad_first_bias: float32 [16], replicated
- grad_second_kernel: float32 [128, 16, 3, 3, 3], replicated
- grad_second_bias: float32 [128], replicated
- grad_head_weight: float32 [4, 128], replicated
- grad_head_bias: float32 [4], replicated
All inputs are finite; a program needn't handle non-finite values.
Results may differ from a plain program's by a relative error of at most 0.0034.
Values may be sent and summed in bfloat16 or wider, within the bound.
A program may use at most 128 MiB of HBM per device.

v0:
```python
import functools

import jax
import jax.numpy as jnp
from jax import lax
from jax.experimental import pallas as pl
from jax.experimental.pallas import tpu as pltpu
from jax.sharding import PartitionSpec as P

F32 = jnp.float32
BF16 = jnp.bfloat16
MESH = pl.DeviceIdType.MESH
NT = (((1,), (1,)), ((), ()))
TN = (((0,), (0,)), ((), ()))
EARLY = 448
ROWS = 624


def iota(shape, dim):
    return lax.broadcasted_iota(jnp.int32, shape, dim)


def dot(a, b, dims=(((1,), (0,)), ((), ())), precision=None):
    return lax.dot_general(a, b, dims, precision=precision, preferred_element_type=F32)


def to_column(row):
    n = row.shape[1]
    return jnp.sum(jnp.where(iota((n, n), 0) == iota((n, n), 1), row, 0.0), axis=1, keepdims=True)


def to_row(column):
    n = column.shape[0]
    return jnp.sum(jnp.where(iota((n, n), 0) == iota((n, n), 1), column, 0.0), axis=0, keepdims=True)


def shifted(block, dz):
    if dz == 1:
        return block
    lane = iota(block.shape, 1)
    if dz == 0:
        return jnp.where(lane == 0, 0.0, pltpu.roll(block, 1, 1))
    return jnp.where(lane == 127, 0.0, pltpu.roll(block, 127, 1))


def kernel(
    n, nd,
    vol, tgt, k1m, b1, k2t, b2, hw, hb,
    pred_o, gk1_o, gb1_o, gk2_o, gb2_o, gh_o, ghb_o,
    lo1, hi1, lo2, hi2, patch, patch3, w1, own1, pz, p2, mk, mo, zs, ga, gg, acc1,
    fbuf, buf, rsbuf, dpbuf, res,
    h_send, h_recv, f_send, f_recv, r_send, r_recv, d_send, d_recv, g_send, g_recv,
):
    me = lax.axis_index("space")
    md = lax.axis_index("dp")
    samples = nd
    cells_two = 2 * 8 * 128 * n
    shard = buf.shape[0] // n

    def peer(j):
        return lax.rem(me + j, n)

    def dpeer(j):
        return lax.rem(md + j, nd)

    barrier = pltpu.get_barrier_semaphore()
    for j in range(1, n):
        pl.semaphore_signal(barrier, inc=1, device_id={"space": peer(j)}, device_id_type=MESH)
    for j in range(1, nd):
        pl.semaphore_signal(barrier, inc=1, device_id={"dp": dpeer(j)}, device_id_type=MESH)

    def remote(src, dst, send, recv, axis, to):
        return pltpu.make_async_remote_copy(
            src_ref=src, dst_ref=dst, send_sem=send, recv_sem=recv,
            device_id={axis: to}, device_id_type=MESH,
        )

    split = (iota((256, 512), 0) == 2 * (iota((256, 512), 1) & 127) + (iota((256, 512), 1) >> 7) - 1)
    split = split.astype(F32).astype(BF16)

    def place(blocks, first):
        rows = jnp.concatenate([blk.reshape(64, 256) for blk in blocks], axis=0)
        parts = dot(rows, split).astype(BF16)
        for i in range(len(blocks)):
            for s in range(4):
                patch[s * 64:(s + 1) * 64, (first + i) * 128:(first + i + 1) * 128] = (
                    parts[i * 64:(i + 1) * 64, s * 128:(s + 1) * 128]
                )

    pl.semaphore_wait(barrier, n - 1 + nd - 1)

    first = [vol, vol, vol.at[:, 3:4], vol.at[:, 0:1]]
    into = [lo1, hi1, lo2, hi2]
    steps = [1, -1, 2, -2]
    halo = [
        remote(first[i], into[i], h_send.at[i], h_recv.at[i], "space", lax.rem(me + steps[i] + n, n))
        for i in range(4)
    ]
    has_to = [me < n - 1, me > 0, me < n - 2, me > 1]
    has_from = [me > 0, me < n - 1, me > 1, me < n - 2]
    for i in range(4):
        pl.when(has_to[i])(halo[i].start)
    for i in range(4):
        @pl.when(jnp.logical_not(has_from[i]))
        def _(i=i):
            into[i][...] = jnp.zeros_like(into[i])

    place([vol[:, x] for x in range(4)], 5)

    col = iota((12, 512), 1)
    tap = iota((12, 512), 0)
    pick = (((col & 63) >> 4) == (tap & 3)) & (((col & 255) >> 6) == (col >> 8) + (tap >> 2))
    spread = dot(k1m[...], pick.astype(F32).astype(BF16))
    ycol = iota((16, 256), 1) & 15
    for dx in range(3):
        for p in range(2):
            e = [spread[(dx * 3 + dy) * 16:(dx * 3 + dy + 1) * 16, p * 256:(p + 1) * 256] for dy in range(3)]
            for q in range(2):
                for yh in range(8):
                    y = 2 * yh + q
                    block = jnp.where(
                        ycol == y - 1, e[0],
                        jnp.where(ycol == y, e[1], jnp.where(ycol == y + 1, e[2], 0.0)),
                    )
                    r = p * 256 + (q * 8 + yh) * 16
                    w1[r:r + 16, dx * 256:(dx + 1) * 256] = block.astype(BF16)
    bias1 = jnp.broadcast_to(to_column(b1[...]), (16, 128))
    bias1 = jnp.concatenate([bias1] * 8, axis=0)
    bias2 = jnp.broadcast_to(to_column(b2[...]), (128, 128))

    pz[:, 0:16, :] = jnp.zeros((3, 16, 768), BF16)
    pz[:, 144:160, :] = jnp.zeros((3, 16, 768), BF16)
    p2[432:448, :] = jnp.ones((16, 4096), BF16)
    own = ((iota((128, 512), 1) >= 128) & (iota((128, 512), 1) < 384)).astype(F32)
    for y in range(8):
        mo[128:256, y * 512:(y + 1) * 512] = own.astype(BF16)
    buf[ROWS - 16:, :] = jnp.zeros((buf.shape[0] - ROWS + 16, 128), F32)

    for i in range(4):
        pl.when(has_from[i])(halo[i].wait_recv)
    place([lo2[:, 0]] + [lo1[:, x] for x in range(4)], 0)
    place([hi1[:, x] for x in range(4)] + [hi2[:, 0]], 9)
    for dx in range(3):
        patch3[dx * 256:(dx + 1) * 256, :] = patch[:, dx * 128:dx * 128 + 1536]

    low_ok = jnp.where(me > 0, 1.0, 0.0).astype(F32)
    high_ok = jnp.where(me < n - 1, 1.0, 0.0).astype(F32)
    for xp in range(6):
        pre = dot(w1[...], patch3[:, xp * 256:(xp + 1) * 256])
        total = None
        for r in range(4):
            for x in range(2):
                part = pre[r * 128:(r + 1) * 128, x * 128:(x + 1) * 128] + bias1
                if 2 <= xp < 4:
                    c = (xp - 2) * 256 + x * 128
                    own1[r * 128:(r + 1) * 128, c:c + 128] = part
                part = jnp.where(part > 0, part, 0.3 * part)
                total = part if total is None else total + part
        total = total * 0.125
        if xp < 2:
            total = total * low_ok
        if xp > 3:
            total = total * high_ok
        for dz in range(3):
            pz[dz, 16:144, xp * 128:(xp + 1) * 128] = shifted(total, dz).astype(BF16)

    for dx in range(3):
        for dy in range(3):
            for dz in range(3):
                t = (dx * 3 + dy) * 3 + dz
                for y in range(8):
                    p2[t * 16:(t + 1) * 16, y * 512:(y + 1) * 512] = (
                        pz[dz, (y + dy) * 16:(y + dy + 1) * 16, dx * 128:dx * 128 + 512]
                    )

    fsum = jnp.zeros((128, 128), F32)
    for y in range(8):
        pre = dot(k2t[...], p2[0:432, y * 512:(y + 1) * 512], TN)
        for x in range(4):
            lanes = slice(y * 512 + x * 128, y * 512 + (x + 1) * 128)
            part = pre[:, x * 128:(x + 1) * 128] + bias2
            mask = jnp.where(part > 0, 1.0, 0.0)
            mk[:, lanes] = mask.astype(BF16)
            if 1 <= x < 3:
                fsum = fsum + jnp.where(part > 0, part, 0.3 * part)
                mo[0:128, lanes] = mask.astype(BF16)
            else:
                mo[0:128, lanes] = jnp.zeros((128, 128), BF16)

    frow = jnp.sum(fsum.T, axis=0, keepdims=True)
    fbuf[me] = jnp.broadcast_to(frow, (8, 128))
    feats = [
        remote(fbuf.at[me], fbuf.at[me], f_send.at[j], f_recv.at[me], "space", peer(j))
        for j in range(1, n)
    ]
    for copy in feats:
        copy.start()

    sums = dot(p2[...], mo[...], NT)

    def arrived(slots, sems, axis, source):
        remote(slots.at[source], slots.at[source], f_send.at[0], sems.at[source], axis, source).wait_recv()

    for j in range(1, n):
        arrived(fbuf, f_recv, "space", peer(j))
    total = fbuf[0]
    for s in range(1, n):
        total = total + fbuf[s]
    features = total[0:4] / cells_two
    head = hw[...]
    prediction = jnp.sum(head * features, axis=1, keepdims=True) + to_column(hb[...])
    grad_pred = 2.0 * (prediction - to_column(tgt[...])) / samples
    pred_o[...] = to_row(prediction)
    scaled = jnp.sum(head * grad_pred, axis=0, keepdims=True) / cells_two
    plus = scaled.astype(BF16).astype(F32)
    minus = (0.3 * scaled).astype(BF16).astype(F32)
    leader = jnp.where(me == 0, 1.0, 0.0).astype(F32)

    buf[0:EARLY, :] = sums[:, 128:256] * minus + sums[:, 0:128] * (plus - minus)
    buf[608:612, :] = leader * (grad_pred * features)
    buf[616:620, :] = leader * jnp.broadcast_to(grad_pred, (4, 128))

    whole = EARLY // shard
    scatter = [
        remote(
            buf.at[pl.ds(pl.multiple_of(peer(j) * shard, 8), shard)], rsbuf.at[me],
            r_send.at[j], r_recv.at[me], "space", peer(j),
        )
        for j in range(1, n)
    ]
    for j in range(1, n):
        pl.when(peer(j) < whole)(scatter[j - 1].start)

    plus_c = jnp.broadcast_to(plus, (128, 128)).T
    minus_c = jnp.broadcast_to(minus, (128, 128)).T
    for y in range(8):
        parts = []
        for x in range(4):
            part = mk[:, y * 512 + x * 128:y * 512 + (x + 1) * 128].astype(F32)
            part = jnp.where(part > 0, plus_c, minus_c)
            if x == 0:
                part = part * low_ok
            if x == 3:
                part = part * high_ok
            parts.append(part.astype(BF16))
        zs[:, y * 512:(y + 1) * 512] = dot(k2t[...], jnp.concatenate(parts, axis=1))
    for y in range(8):
        for dz in range(3):
            total = None
            for dx in range(3):
                for dy in range(3):
                    ys = y + 1 - dy
                    if 0 <= ys < 8:
                        t = (dx * 3 + dy) * 3 + dz
                        c = ys * 512 + (2 - dx) * 128
                        part = zs[t * 16:(t + 1) * 16, c:c + 256]
                        total = part if total is None else total + part
            ga[dz, y * 16:(y + 1) * 16, :] = total
    bsum = jnp.zeros((16, 128), F32)
    for xp in range(2):
        lanes = slice(xp * 128, (xp + 1) * 128)
        g = shifted(ga[0, :, lanes], 2) + ga[1, :, lanes] + shifted(ga[2, :, lanes], 0)
        g = g * 0.125
        low = 0.3 * g
        for r in range(4):
            for x in range(2):
                c = xp * 256 + x * 128
                part = jnp.where(own1[r * 128:(r + 1) * 128, c:c + 128] > 0, g, low).astype(BF16)
                gg[r * 128:(r + 1) * 128, c:c + 128] = part
                part = part.astype(F32)
                for k in range(8):
                    bsum = bsum + part[k * 16:(k + 1) * 16]
    for dx in range(3):
        full = dot(gg[...], patch3[dx * 256:(dx + 1) * 256, 512:1024], NT)
        for p in range(2):
            accs = [jnp.zeros((16, 256), F32)] * 3
            for q in range(2):
                for yh in range(8):
                    y = 2 * yh + q
                    r = p * 256 + (q * 8 + yh) * 16
                    block = full[r:r + 16, :]
                    for dy in range(3):
                        accs[dy] = accs[dy] + jnp.where(ycol == y + dy - 1, block, 0.0)
            for dy in range(3):
                r = (dx * 3 + dy) * 16
                acc1[r:r + 16, p * 256:(p + 1) * 256] = accs[dy]
    col = iota((128, 512), 1)
    tap = iota((128, 512), 0)
    pick = (((col & 63) >> 4) == (tap & 3)) & (((col & 255) >> 6) == (col >> 8) + (tap >> 2)) & (tap < 12)
    buf[448:592, :] = dot(acc1[...], pick.astype(F32), NT, lax.Precision.HIGHEST)
    buf[592:608, :] = bsum
    for j in range(1, n):
        pl.when(peer(j) >= whole)(scatter[j - 1].start)

    for j in range(1, n):
        arrived(rsbuf, r_recv, "space", peer(j))
    rsbuf[me] = buf[pl.ds(pl.multiple_of(me * shard, 8), shard), :]
    total = rsbuf[0]
    for s in range(1, n):
        total = total + rsbuf[s]
    dpbuf[md] = total
    across = [
        remote(dpbuf.at[md], dpbuf.at[md], d_send.at[j], d_recv.at[md], "dp", dpeer(j))
        for j in range(1, nd)
    ]
    for copy in across:
        copy.start()
    for j in range(1, nd):
        arrived(dpbuf, d_recv, "dp", dpeer(j))
    total = dpbuf[0]
    for s in range(1, nd):
        total = total + dpbuf[s]
    mine = pl.ds(pl.multiple_of(me * shard, 8), shard)
    res[mine, :] = total
    gather = [
        remote(res.at[mine], res.at[mine], g_send.at[j], g_recv.at[me], "space", peer(j))
        for j in range(1, n)
    ]
    for copy in gather:
        copy.start()
    for j in range(1, n):
        source = peer(j)
        part = res.at[pl.ds(pl.multiple_of(source * shard, 8), shard)]
        remote(part, part, f_send.at[0], g_recv.at[source], "space", source).wait_recv()

    gk2_o[...] = res[0:432, :]
    gb2_o[...] = res[432:433, :]
    gk1_o[...] = res[448:592, 0:12]
    gb1_o[...] = to_row(jnp.sum(res[592:608, :], axis=1, keepdims=True))
    gh_o[...] = res[608:612, :]
    ghb_o[...] = to_row(res[616:620, 0:1])

    for i in range(4):
        pl.when(has_to[i])(halo[i].wait_send)
    for copy in feats + scatter + across + gather:
        copy.wait_send()


def body(
    volumes, targets, first_kernel, first_bias, second_kernel, second_bias, head_weight, head_bias
):
    n = lax.axis_size("space")
    nd = lax.axis_size("dp")
    shard = -(-ROWS // (8 * n)) * 8
    k1m = first_kernel.transpose(2, 3, 0, 4, 1).reshape(144, 12)
    k2t = second_kernel.transpose(2, 3, 4, 1, 0).reshape(432, 128)
    shape = jax.ShapeDtypeStruct
    sem = pltpu.SemaphoreType.DMA
    v = pltpu.VMEM
    pred, gk1, gb1, gk2, gb2, gh, ghb = pl.pallas_call(
        functools.partial(kernel, n, nd),
        out_shape=(
            shape((1, 4), F32), shape((144, 12), F32), shape((1, 16), F32), shape((432, 128), F32),
            shape((1, 128), F32), shape((4, 128), F32), shape((1, 4), F32),
        ),
        in_specs=[pl.BlockSpec(memory_space=pltpu.VMEM)] * 8,
        out_specs=[pl.BlockSpec(memory_space=pltpu.VMEM)] * 7,
        scratch_shapes=[
            v((4, 4, 16, 256), BF16), v((4, 4, 16, 256), BF16),
            v((4, 1, 16, 256), BF16), v((4, 1, 16, 256), BF16),
            v((256, 1792), BF16), v((768, 1536), BF16), v((512, 768), BF16), v((512, 512), F32),
            v((3, 160, 768), BF16), v((448, 4096), BF16), v((128, 4096), BF16), v((256, 4096), BF16),
            v((432, 4096), F32), v((3, 128, 256), F32), v((512, 512), BF16), v((144, 512), F32),
            v((n, 8, 128), F32), v((n * shard, 128), F32), v((n, shard, 128), F32),
            v((nd, shard, 128), F32), v((n * shard, 128), F32),
            sem((4,)), sem((4,)), sem((n,)), sem((n,)), sem((n,)), sem((n,)),
            sem((nd,)), sem((nd,)), sem((n,)), sem((n,)),
        ],
        compiler_params=pltpu.CompilerParams(
            collective_id=0, has_side_effects=True, vmem_limit_bytes=56 * 1024 * 1024
        ),
        cost_estimate=pl.CostEstimate(flops=5_000_000_000, bytes_accessed=2_000_000, transcendentals=0),
    )(
        volumes[0], targets, k1m, first_bias[None], k2t, second_bias[None], head_weight, head_bias[None]
    )
    gk1 = gk1.reshape(3, 3, 16, 3, 4).transpose(2, 4, 0, 1, 3)
    gk2 = gk2.reshape(3, 3, 3, 16, 128).transpose(4, 3, 0, 1, 2)
    return pred, gk1, gb1[0], gk2, gb2[0], gh, ghb[0]


def solution(mesh):
    in_specs = (P("dp", None, "space", None, None), P("dp", None), P(), P(), P(), P(), P(), P())
    out_specs = (P("dp", None), P(), P(), P(), P(), P(), P())
    return jax.shard_map(body, mesh=mesh, in_specs=in_specs, out_specs=out_specs, check_vma=False)
```

profile of v0, /device:TPU:0, one launch (start us, length us, event | category | flops | bytes accessed | tf_op | source)
XLA Modules:
  0.0 44.3 jit_solution(480728218947101100)
XLA Ops:
  0.6 0.8 %copy.17 = bf16[3,3,16,3,4]{2,1,0,4,3:T(4,128)(2,1)S(1)} copy(bf16[3,3,16,3,4]{2,4,3,1,0:T(4,128)(2,1)} %bitcast.21) | data formatting | bytes 6912 | tf_op jit(solution)/shard_map/transpose | solution.py:345
  1.4 0.1 reshape.26
  1.5 0.7 %copy.18.k1m = bf16[144,12]{1,0:T(8,128)(2,1)} copy(bf16[144,12]{0,1:T(8,128)(2,1)S(1)} %reshape.26) | data formatting | bytes 6912 | tf_op jit(solution)/shard_map/reshape | solution.py:345
  2.2 36.8 %shard_map.135 = (f32[1,4]{1,0:T(1,128)}, f32[144,12]{1,0:T(8,128)}, f32[1,16]{1,0:T(1,128)}, f32[432,128]{1,0:T(8,128)}, f32[1,128]{1,0:T(1,128)}, /*index=5*/f32[4,128]{1,0:T(4,128)}, f32[1,4]{1,0:T(1,128)}) custom-call(bf16[4,4,16,256]{3,2,1,0:T(8,128)(2,1)} %bitcast.22, f32[1,4]{1,0:T(1,128)} %tgt.1, bf16[144,12]{1,0:T(8,128)(2,1)} %copy.18.k1m, ...), custom_call_target="tpu_custom_call" | custom-call | flops 5000000000 | bytes 2000000 | tf_op jit(solution)/shard_map/pallas_call | solution.py:350
  39.0 0.0 copy-start
  39.0 1.0 %copy.19 = f32[144,12]{0,1:T(8,128)S(1)} copy(f32[144,12]{1,0:T(8,128)} %get-tuple-element.15) | data formatting | bytes 13824 | tf_op jit(solution)/shard_map/pallas_call | solution.py:350
  40.0 0.1 reshape.28
  40.1 0.0 copy-start.5
  40.2 0.6 %copy.20 = f32[16,4,3,3,3]{0,1,4,3,2:T(4,128)} copy(f32[16,4,3,3,3]{0,3,2,1,4:T(4,128)S(1)} %bitcast.19) | data formatting | bytes 13824
  40.8 0.0 copy-done.5
  40.8 0.0 copy-start.4
  40.8 0.5 %copy.27 = f32[1,4]{1,0:T(1,128)} copy(f32[1,4]{1,0:T(1,128)S(1)} %copy-done.5) | data formatting | bytes 32
  41.3 0.2 copy-done.4
  41.5 0.5 %copy.28 = f32[16]{0:T(128)} copy(f32[16]{0:T(128)S(1)} %bitcast.29) | data formatting | bytes 128
  42.0 0.0 copy-done
  42.0 0.0 copy-start.3
  42.0 0.7 %copy.29 = f32[128,16,3,3,3]{0,1,4,3,2:T(8,128)} copy(f32[128,16,3,3,3]{0,1,4,3,2:T(8,128)S(1)} %bitcast.20) | data formatting | bytes 442368
  42.7 0.0 copy-done.3
  42.7 0.5 %copy.30 = f32[128]{0:T(128)} copy(f32[128]{0:T(128)S(1)} %bitcast.28) | data formatting | bytes 1024
  43.2 0.0 copy-done.1
  43.2 0.0 copy-start.2
  43.2 0.6 %copy.31 = f32[4,128]{1,0:T(4,128)} copy(f32[4,128]{1,0:T(4,128)S(1)} %copy-done.1) | data formatting | bytes 4096
  43.8 0.0 copy-done.2
  43.8 0.5 %copy.32 = f32[4]{0:T(128)} copy(f32[4]{0:T(128)S(1)} %bitcast.27) | data formatting | bytes 32
  (1 shorter events, 0.0 us)
Async XLA Ops:
  39.0 3.0 %copy-start = (f32[432,128]{1,0:T(8,128)S(1)}, f32[432,128]{1,0:T(8,128)}, u32[]{:S(2)}) copy-start(f32[432,128]{1,0:T(8,128)} %get-tuple-element.17) | copy-start | bytes 663556
  40.1 0.7 %copy-start.5 = (f32[1,4]{1,0:T(1,128)S(1)}, f32[1,4]{1,0:T(1,128)}, u32[]{:S(2)}) copy-start(f32[1,4]{1,0:T(1,128)} %get-tuple-element.35) | copy-start | bytes 52
  40.8 0.7 %copy-start.4 = (f32[1,16]{1,0:T(1,128)S(1)}, f32[1,16]{1,0:T(1,128)}, u32[]{:S(2)}) copy-start(f32[1,16]{1,0:T(1,128)} %get-tuple-element.16) | copy-start | bytes 196
  42.0 0.7 %copy-start.3 = (f32[1,128]{1,0:T(1,128)S(1)}, f32[1,128]{1,0:T(1,128)}, u32[]{:S(2)}) copy-start(f32[1,128]{1,0:T(1,128)} %get-tuple-element.18) | copy-start | bytes 1540
  42.0 1.2 %copy-start.1 = (f32[4,128]{1,0:T(4,128)S(1)}, f32[4,128]{1,0:T(4,128)}, u32[]{:S(2)}) copy-start(f32[4,128]{1,0:T(4,128)} %get-tuple-element.40) | copy-start | bytes 6148
  43.2 0.6 %copy-start.2 = (f32[1,4]{1,0:T(1,128)S(1)}, f32[1,4]{1,0:T(1,128)}, u32[]{:S(2)}) copy-start(f32[1,4]{1,0:T(1,128)} %get-tuple-element.20) | copy-start | bytes 52
where the time goes:
time: 44.8 us; the launch traced here: 44.3 us
  Pallas kernels  36.8 us (82%)
  local copies, waits for them, and re-layouts  6.86 us (15%)
  between operations  0.68 us (2%)
    pallas_call x1, Pallas kernels, body(): pl.pallas_call(functools.partial(kernel, n, nd), out_shape=(shape((1, 4),...  36.8 us
    unnamed x19, local copies, waits for them, and re-layouts  4.16 us
    pallas_call x1, local copies, waits for them, and re-layouts, body(): pl.pallas_call(functools.partial(kernel, n, nd), out_shape=(shape((1, 4),...  1 us

commit v1 on v0

--- a/solution.py
+++ b/solution.py
@@ -13,7 +13,7 @@
 NT = (((1,), (1,)), ((), ()))
 TN = (((0,), (0,)), ((), ()))
 EARLY = 448
-ROWS = 624
+ROWS = 512
 
 
 def iota(shape, dim):
@@ -45,10 +45,10 @@
 
 def kernel(
     n, nd,
-    vol, tgt, k1m, b1, k2t, b2, hw, hb,
-    pred_o, gk1_o, gb1_o, gk2_o, gb2_o, gh_o, ghb_o,
-    lo1, hi1, lo2, hi2, patch, patch3, w1, own1, pz, p2, mk, mo, zs, ga, gg, acc1,
-    fbuf, buf, rsbuf, dpbuf, res,
+    vol, tgt, k1, b1, k2t, b2, hw, hb,
+    res, pred_o,
+    k1s, lo1, hi1, lo2, hi2, patch, patch3, w1, own1, pz, p2, mk, mo, zs, ga, gg, acc1,
+    fbuf, buf, rsbuf, dpbuf,
     h_send, h_recv, f_send, f_recv, r_send, r_recv, d_send, d_recv, g_send, g_recv,
 ):
     me = lax.axis_index("space")
@@ -110,7 +110,10 @@
     col = iota((12, 512), 1)
     tap = iota((12, 512), 0)
     pick = (((col & 63) >> 4) == (tap & 3)) & (((col & 255) >> 6) == (col >> 8) + (tap >> 2))
-    spread = dot(k1m[...], pick.astype(F32).astype(BF16))
+    for t in range(9):
+        for dz in range(3):
+            k1s[dz * 4:(dz + 1) * 4, t * 16:(t + 1) * 16] = k1[t * 3 + dz].astype(F32)
+    spread = dot(k1s[0:12, 0:144].astype(BF16), pick.astype(F32).astype(BF16), TN)
     ycol = iota((16, 256), 1) & 15
     for dx in range(3):
         for p in range(2):
@@ -134,7 +137,7 @@
     own = ((iota((128, 512), 1) >= 128) & (iota((128, 512), 1) < 384)).astype(F32)
     for y in range(8):
         mo[128:256, y * 512:(y + 1) * 512] = own.astype(BF16)
-    buf[ROWS - 16:, :] = jnp.zeros((buf.shape[0] - ROWS + 16, 128), F32)
+    buf[EARLY:, :] = jnp.zeros((buf.shape[0] - EARLY, 128), F32)
 
     for i in range(4):
         pl.when(has_from[i])(halo[i].wait_recv)
@@ -210,15 +213,15 @@
     head = hw[...]
     prediction = jnp.sum(head * features, axis=1, keepdims=True) + to_column(hb[...])
     grad_pred = 2.0 * (prediction - to_column(tgt[...])) / samples
-    pred_o[...] = to_row(prediction)
+    pred_o[...] = jnp.broadcast_to(prediction, (4, 128))
     scaled = jnp.sum(head * grad_pred, axis=0, keepdims=True) / cells_two
     plus = scaled.astype(BF16).astype(F32)
     minus = (0.3 * scaled).astype(BF16).astype(F32)
     leader = jnp.where(me == 0, 1.0, 0.0).astype(F32)
 
     buf[0:EARLY, :] = sums[:, 128:256] * minus + sums[:, 0:128] * (plus - minus)
-    buf[608:612, :] = leader * (grad_pred * features)
-    buf[616:620, :] = leader * jnp.broadcast_to(grad_pred, (4, 128))
+    buf[496:500, :] = leader * (grad_pred * features)
+    buf[504:508, :] = leader * jnp.broadcast_to(grad_pred, (4, 128))
 
     whole = EARLY // shard
     scatter = [
@@ -284,11 +287,13 @@
             for dy in range(3):
                 r = (dx * 3 + dy) * 16
                 acc1[r:r + 16, p * 256:(p + 1) * 256] = accs[dy]
-    col = iota((128, 512), 1)
-    tap = iota((128, 512), 0)
+    col = iota((16, 512), 1)
+    tap = iota((16, 512), 0)
     pick = (((col & 63) >> 4) == (tap & 3)) & (((col & 255) >> 6) == (col >> 8) + (tap >> 2)) & (tap < 12)
-    buf[448:592, :] = dot(acc1[...], pick.astype(F32), NT, lax.Precision.HIGHEST)
-    buf[592:608, :] = bsum
+    first = dot(pick.astype(F32), acc1[...], NT, lax.Precision.HIGHEST)
+    buf[448:464, :] = first[:, 0:128]
+    buf[464:480, 0:16] = first[:, 128:144]
+    buf[480:496, :] = jnp.broadcast_to(jnp.sum(bsum, axis=1, keepdims=True), (16, 128))
     for j in range(1, n):
         pl.when(peer(j) >= whole)(scatter[j - 1].start)
 
@@ -310,8 +315,8 @@
     total = dpbuf[0]
     for s in range(1, nd):
         total = total + dpbuf[s]
-    mine = pl.ds(pl.multiple_of(me * shard, 8), shard)
-    res[mine, :] = total
+    mine = pl.ds(pl.multiple_of(me * shard, 16), shard)
+    res[mine, :] = total.astype(BF16)
     gather = [
         remote(res.at[mine], res.at[mine], g_send.at[j], g_recv.at[me], "space", peer(j))
         for j in range(1, n)
@@ -320,20 +325,27 @@
         copy.start()
     for j in range(1, n):
         source = peer(j)
-        part = res.at[pl.ds(pl.multiple_of(source * shard, 8), shard)]
+        part = res.at[pl.ds(pl.multiple_of(source * shard, 16), shard)]
         remote(part, part, f_send.at[0], g_recv.at[source], "space", source).wait_recv()
-
-    gk2_o[...] = res[0:432, :]
-    gb2_o[...] = res[432:433, :]
-    gk1_o[...] = res[448:592, 0:12]
-    gb1_o[...] = to_row(jnp.sum(res[592:608, :], axis=1, keepdims=True))
-    gh_o[...] = res[608:612, :]
-    ghb_o[...] = to_row(res[616:620, 0:1])
 
     for i in range(4):
         pl.when(has_to[i])(halo[i].wait_send)
     for copy in feats + scatter + across + gather:
         copy.wait_send()
+
+
+def finish(res, pred, pred_o, gk1_o, gb1_o, gk2_o, gb2_o, gh_o, ghb_o):
+    gk2_o[...] = res[0:432, :].astype(F32)
+    rest = res[432:512, :].astype(F32)
+    gb2_o[...] = rest[0:1]
+    for t in range(9):
+        r, c = (16, t * 16) if t < 8 else (32, 0)
+        for dz in range(3):
+            gk1_o[t * 3 + dz] = rest[r + dz * 4:r + (dz + 1) * 4, c:c + 16]
+    gb1_o[...] = to_row(rest[48:64, 0:1])
+    gh_o[...] = rest[64:68]
+    ghb_o[...] = to_row(rest[72:76, 0:1])
+    pred_o[...] = to_row(pred[:, 0:1])
 
 
 def body(
@@ -341,28 +353,26 @@
 ):
     n = lax.axis_size("space")
     nd = lax.axis_size("dp")
-    shard = -(-ROWS // (8 * n)) * 8
-    k1m = first_kernel.transpose(2, 3, 0, 4, 1).reshape(144, 12)
+    shard = -(-ROWS // (16 * n)) * 16
+    k1 = first_kernel.transpose(2, 3, 4, 1, 0).reshape(27, 4, 16)
     k2t = second_kernel.transpose(2, 3, 4, 1, 0).reshape(432, 128)
     shape = jax.ShapeDtypeStruct
     sem = pltpu.SemaphoreType.DMA
     v = pltpu.VMEM
-    pred, gk1, gb1, gk2, gb2, gh, ghb = pl.pallas_call(
+    res, pred = pl.pallas_call(
         functools.partial(kernel, n, nd),
-        out_shape=(
-            shape((1, 4), F32), shape((144, 12), F32), shape((1, 16), F32), shape((432, 128), F32),
-            shape((1, 128), F32), shape((4, 128), F32), shape((1, 4), F32),
-        ),
+        out_shape=(shape((n * shard, 128), BF16), shape((4, 128), F32)),
         in_specs=[pl.BlockSpec(memory_space=pltpu.VMEM)] * 8,
-        out_specs=[pl.BlockSpec(memory_space=pltpu.VMEM)] * 7,
+        out_specs=[pl.BlockSpec(memory_space=pltpu.VMEM)] * 2,
         scratch_shapes=[
+            v((16, 256), F32),
             v((4, 4, 16, 256), BF16), v((4, 4, 16, 256), BF16),
             v((4, 1, 16, 256), BF16), v((4, 1, 16, 256), BF16),
             v((256, 1792), BF16), v((768, 1536), BF16), v((512, 768), BF16), v((512, 512), F32),
             v((3, 160, 768), BF16), v((448, 4096), BF16), v((128, 4096), BF16), v((256, 4096), BF16),
             v((432, 4096), F32), v((3, 128, 256), F32), v((512, 512), BF16), v((144, 512), F32),
             v((n, 8, 128), F32), v((n * shard, 128), F32), v((n, shard, 128), F32),
-            v((nd, shard, 128), F32), v((n * shard, 128), F32),
+            v((nd, shard, 128), F32),
             sem((4,)), sem((4,)), sem((n,)), sem((n,)), sem((n,)), sem((n,)),
             sem((nd,)), sem((nd,)), sem((n,)), sem((n,)),
         ],
@@ -371,9 +381,18 @@
         ),
         cost_estimate=pl.CostEstimate(flops=5_000_000_000, bytes_accessed=2_000_000, transcendentals=0),
     )(
-        volumes[0], targets, k1m, first_bias[None], k2t, second_bias[None], head_weight, head_bias[None]
+        volumes[0], targets, k1, first_bias[None], k2t, second_bias[None], head_weight, head_bias[None]
     )
-    gk1 = gk1.reshape(3, 3, 16, 3, 4).transpose(2, 4, 0, 1, 3)
+    pred, gk1, gb1, gk2, gb2, gh, ghb = pl.pallas_call(
+        finish,
+        out_shape=(
+            shape((1, 4), F32), shape((27, 4, 16), F32), shape((1, 16), F32), shape((432, 128), F32),
+            shape((1, 128), F32), shape((4, 128), F32), shape((1, 4), F32),
+        ),
+        in_specs=[pl.BlockSpec(memory_space=pltpu.VMEM)] * 2,
+        out_specs=[pl.BlockSpec(memory_space=pltpu.VMEM)] * 7,
+    )(res, pred)
+    gk1 = gk1.reshape(3, 3, 3, 4, 16).transpose(4, 3, 0, 1, 2)
     gk2 = gk2.reshape(3, 3, 3, 16, 128).transpose(4, 3, 0, 1, 2)
     return pred, gk1, gb1[0], gk2, gb2[0], gh, ghb[0]
 

time: 44.8 us -> 35.1 us (0.78)
  local copies, waits for them, and re-layouts: 6.86 us -> 0 us
  Pallas kernels: 36.8 us -> 34.3 us
    unnamed x19 -> x0, local copies, waits for them, and re-layouts: 4.16 us -> none
    pallas_call x1 -> x2, Pallas kernels: 36.8 us -> 34.3 us  [the longest x1 32.7 us: body(): pl.pallas_call(functools.partial(kernel, n, nd), out_shape=(shape((n * sh...]
    pallas_call x1 -> x0, local copies, waits for them, and re-layouts: 1 us -> none  [body(): pl.pallas_call(functools.partial(kernel, n, nd), out_shape=(shape((1, 4),...]
    reshape x3 -> x0, local copies, waits for them, and re-layouts: 0.94 us -> none  [the longest x2 0.83 us: body(): k1m = first_kernel.transpose(2, 3, 0, 4, 1).reshape(144, 12)]
    transpose x1 -> x0, local copies, waits for them, and re-layouts: 0.76 us -> none  [body(): k1m = first_kernel.transpose(2, 3, 0, 4, 1).reshape(144, 12)]
where the time goes in v1:
time: 35.1 us; the launch traced here: 35 us
  Pallas kernels  34.3 us (98%)
  between operations  0.64 us (2%)
    pallas_call x1, Pallas kernels, body(): pl.pallas_call(functools.partial(kernel, n, nd), out_shape=(shape((n * sh...  32.7 us
    pallas_call x1, Pallas kernels, body(): pl.pallas_call(finish, out_shape=(shape((1, 4), F32), shape((27, 4, 16),...  1.64 us

profile of v1, /device:TPU:0, one launch (start us, length us, event | category | flops | bytes accessed | tf_op | source)
XLA Modules:
  0.0 35.0 jit_solution(7812962170140845042)
XLA Ops:
  0.6 32.7 %shard_map.135 = (bf16[512,128]{1,0:T(8,128)(2,1)}, f32[4,128]{1,0:T(4,128)}) custom-call(bf16[4,4,16,256]{3,2,1,0:T(8,128)(2,1)} %bitcast.20, f32[1,4]{1,0:T(1,128)} %tgt.1, bf16[27,4,16]{2,1,0:T(4,128)(2,1)} %bitcast.23, f32[1,16]{1,0:T(1,128)} %bitcast.24, bf16[432,128]{1,0:T(8,128)(2,1)} %bitcast.21, f32[1,128]{1,0:T(1,128)} %bitcast.25, f32[4,128]{1,0:T(4,128)} %hw.1, ...), custom_call_target="tpu_custom_call" | custom-call | flops 5000000000 | bytes 2000000 | tf_op jit(solution)/shard_map/pallas_call | solution.py:362
  33.3 1.6 %shard_map.136 = (f32[1,4]{1,0:T(1,128)}, f32[27,4,16]{2,1,0:T(4,128)}, f32[1,16]{1,0:T(1,128)}, f32[432,128]{1,0:T(8,128)}, f32[1,128]{1,0:T(1,128)}, /*index=5*/f32[4,128]{1,0:T(4,128)}, f32[1,4]{1,0:T(1,128)}) custom-call(bf16[512,128]{1,0:T(8,128)(2,1)} %get-tuple-element.16.res, f32[4,128]{1,0:T(4,128)} %get-tuple-element.17.pred), custom_call_target="tpu_custom_call" | custom-call | tf_op jit(solution)/shard_map/pallas_call | solution.py:386

commit v2 on v1

--- a/solution.py
+++ b/solution.py
@@ -273,6 +273,23 @@
                 part = part.astype(F32)
                 for k in range(8):
                     bsum = bsum + part[k * 16:(k + 1) * 16]
+    across = [
+        remote(dpbuf.at[md], dpbuf.at[md], d_send.at[j], d_recv.at[md], "dp", dpeer(j))
+        for j in range(1, nd)
+    ]
+
+    def combine():
+        for j in range(1, n):
+            arrived(rsbuf, r_recv, "space", peer(j))
+        rsbuf[me] = buf[pl.ds(pl.multiple_of(me * shard, 8), shard), :]
+        total = rsbuf[0]
+        for s in range(1, n):
+            total = total + rsbuf[s]
+        dpbuf[md] = total
+        for copy in across:
+            copy.start()
+
+    pl.when(me < whole)(combine)
     for dx in range(3):
         full = dot(gg[...], patch3[dx * 256:(dx + 1) * 256, 512:1024], NT)
         for p in range(2):
@@ -297,19 +314,7 @@
     for j in range(1, n):
         pl.when(peer(j) >= whole)(scatter[j - 1].start)
 
-    for j in range(1, n):
-        arrived(rsbuf, r_recv, "space", peer(j))
-    rsbuf[me] = buf[pl.ds(pl.multiple_of(me * shard, 8), shard), :]
-    total = rsbuf[0]
-    for s in range(1, n):
-        total = total + rsbuf[s]
-    dpbuf[md] = total
-    across = [
-        remote(dpbuf.at[md], dpbuf.at[md], d_send.at[j], d_recv.at[md], "dp", dpeer(j))
-        for j in range(1, nd)
-    ]
-    for copy in across:
-        copy.start()
+    pl.when(me >= whole)(combine)
     for j in range(1, nd):
         arrived(dpbuf, d_recv, "dp", dpeer(j))
     total = dpbuf[0]

time: 35.1 us -> 38.5 us (1.097)
  Pallas kernels: 34.3 us -> 37.7 us
    pallas_call x1, Pallas kernels: 32.7 us -> 36.1 us  [body(): pl.pallas_call(functools.partial(kernel, n, nd), out_shape=(shape((n * sh...]
where the time goes in v2:
time: 38.5 us; the launch traced here: 38.4 us
  Pallas kernels  37.7 us (98%)
  between operations  0.64 us (2%)
    pallas_call x1, Pallas kernels, body(): pl.pallas_call(functools.partial(kernel, n, nd), out_shape=(shape((n * sh...  36.1 us
    pallas_call x1, Pallas kernels, body(): pl.pallas_call(finish, out_shape=(shape((1, 4), F32), shape((27, 4, 16),...  1.64 us

profile of v2, /device:TPU:0, one launch (start us, length us, event | category | flops | bytes accessed | tf_op | source)
XLA Modules:
  0.0 38.4 jit_solution(12698128776347214342)
XLA Ops:
  0.6 36.1 %shard_map.135 = (bf16[512,128]{1,0:T(8,128)(2,1)}, f32[4,128]{1,0:T(4,128)}) custom-call(bf16[4,4,16,256]{3,2,1,0:T(8,128)(2,1)} %bitcast.20, f32[1,4]{1,0:T(1,128)} %tgt.1, bf16[27,4,16]{2,1,0:T(4,128)(2,1)} %bitcast.23, f32[1,16]{1,0:T(1,128)} %bitcast.24, bf16[432,128]{1,0:T(8,128)(2,1)} %bitcast.21, f32[1,128]{1,0:T(1,128)} %bitcast.25, f32[4,128]{1,0:T(4,128)} %hw.1, ...), custom_call_target="tpu_custom_call" | custom-call | flops 5000000000 | bytes 2000000 | tf_op jit(solution)/shard_map/pallas_call | solution.py:367
  36.7 1.6 %shard_map.136 = (f32[1,4]{1,0:T(1,128)}, f32[27,4,16]{2,1,0:T(4,128)}, f32[1,16]{1,0:T(1,128)}, f32[432,128]{1,0:T(8,128)}, f32[1,128]{1,0:T(1,128)}, /*index=5*/f32[4,128]{1,0:T(4,128)}, f32[1,4]{1,0:T(1,128)}) custom-call(bf16[512,128]{1,0:T(8,128)(2,1)} %get-tuple-element.16.res, f32[4,128]{1,0:T(4,128)} %get-tuple-element.17.pred), custom_call_target="tpu_custom_call" | custom-call | tf_op jit(solution)/shard_map/pallas_call | solution.py:391
